TPU v7x, 32 devices: a whole 2x2x4 slice. The times are simulated.
32 devices in a mesh: leaf: 8 (over z, x), obs: 4 (over y, core).
Axes of the slice: x: 2, y: 2, z: 4, core: 2. Of those that a mesh axis runs over, the one named last changes fastest.
Arguments:
- samples_z: bfloat16 [64, 2048], P('obs', 'leaf'), may hold values from -6 to 6
- diag_block: bfloat16 [2048, 256], P('leaf'), as said below
- level_basis: bfloat16 [3, 64, 2048], P(None, None, 'leaf'), may hold values from -6 to 6
- site_xy: float32 [2, 2048], P(None, 'leaf'), may hold values from 0 to 1, as said below
- obs_site: int32 [1024], P('leaf'), may hold values from 0 to 255
- obs_value: float32 [1024], P('leaf'), may hold values from -6 to 6
- obs_count: int32 [8], P('leaf'), may hold values from 1 to 128, 512 in all
- inverse_rows: float32 [512, 512], P(('leaf', 'obs')), may hold values from -0.0078125 to 0.0078125
Outputs:
- conditional: float32 [64, 2048], P('obs', 'leaf')
Inputs may be any that keep to these rules, and one draw needn't show every extreme that they name: `obs_count`: each leaf block's count of observations; the counts sum to 512 and the largest is exactly 128. `obs_site`: slots at or past a block's count are not used. `diag_block`: each leaf block is symmetric. `site_xy`: coordinates lie in the unit square; the sites of each leaf block lie in one cell of a recursive halving of the square that follows the tree of blocks.
All inputs are finite; a program needn't handle non-finite values.
Results may differ from a plain program's by a relative error of at most 0.0003.
Values sent between devices are 32-bit elements; how exact they have to be, the bound alone decides.
A program may use at most 64 MiB of HBM per device.

v0:
```python
import math

import jax
import jax.numpy as jnp
from jax import lax
from jax.sharding import PartitionSpec as P

corr_length = 0.15


def compact_index(counts, slot_count, total):
    inclusive = jnp.cumsum(counts).astype(jnp.int32)
    number = jnp.arange(total, dtype=jnp.int32)
    passed = (inclusive[None, :] <= number[:, None]).astype(jnp.int32)
    owner = jnp.sum(passed, axis=1)
    base = jnp.sum(passed * counts[None, :], axis=1).astype(jnp.int32)
    return owner * slot_count + number - base


def kernel_tile(obs_xy, block_xy):
    delta_x = obs_xy[0][:, None] - block_xy[0][None, :]
    delta_y = obs_xy[1][:, None] - block_xy[1][None, :]
    distance = jnp.sqrt(delta_x * delta_x + delta_y * delta_y)
    return jnp.exp(-distance / corr_length)


def body(samples_z, diag_block, level_basis, site_xy, obs_site, obs_value, obs_count, inverse_rows):
    levels = lax.axis_size("leaf").bit_length() - 1
    leaves = lax.axis_size("leaf")
    sample_dev = samples_z.shape[0]
    site_count = samples_z.shape[1]
    rank = level_basis.shape[1]
    slot_count = obs_site.shape[0]
    total_obs = inverse_rows.shape[1]
    flat_basis = level_basis.reshape(levels * rank, site_count)
    project = lax.dot_general(
        samples_z, flat_basis, (((1,), (1,)), ((), ())), preferred_element_type=jnp.float32
    )
    project = project.reshape(sample_dev, levels, rank)
    depth = jnp.arange(levels, dtype=jnp.int32)
    everyone = lax.all_gather(project[None], "leaf", axis=0, tiled=True)
    position = lax.axis_index("leaf")
    owners = jnp.arange(leaves, dtype=jnp.int32)
    chosen = (owners[None, :] >> depth[:, None] == (position >> depth ^ 1)[:, None]).astype(
        jnp.float32
    )
    siblings = jnp.einsum("jslr,lj->slr", everyone, chosen, precision=lax.Precision.HIGHEST)
    factor = 0.5 / jnp.sqrt(rank * site_count * 2.0 ** depth.astype(jnp.float32))
    coefficients = (siblings * factor[None, :, None]).reshape(sample_dev, levels * rank)
    field = jnp.dot(samples_z, diag_block, preferred_element_type=jnp.float32)
    field = field + jnp.dot(
        coefficients,
        flat_basis,
        precision=lax.Precision.HIGHEST,
        preferred_element_type=jnp.float32,
    )
    residual = obs_value[None, :] - field[:, obs_site]
    local_xy = site_xy[:, obs_site]
    resid_all, xy_all, count_all = (
        lax.all_gather(residual, "leaf", axis=1, tiled=True),
        lax.all_gather(local_xy, "leaf", axis=1, tiled=True),
        lax.all_gather(obs_count, "leaf", axis=0, tiled=True),
    )
    obs_index = compact_index(count_all, slot_count, total_obs)
    resid_comp = resid_all[:, obs_index]
    fold_xy = xy_all[:, obs_index]
    block_rows = lax.all_gather(inverse_rows, "obs", axis=0, tiled=True)
    fold_coef = lax.dot_general(
        resid_comp,
        block_rows,
        (((1,), (1,)), ((), ())),
        precision=lax.Precision.HIGHEST,
        preferred_element_type=jnp.float32,
    )
    empty = jnp.zeros((fold_coef.shape[0], site_count), jnp.float32)
    piece = lax.all_gather(fold_coef, "leaf", axis=1, tiled=True)
    count = piece.shape[1]
    width = math.gcd(count, 1024)

    def one_step(step, running):
        offset = step * width
        part_xy = lax.dynamic_slice_in_dim(fold_xy, offset, width, 1)
        part_coef = lax.dynamic_slice_in_dim(piece, offset, width, 1)
        tile = kernel_tile(part_xy, site_xy)
        return running + jnp.dot(
            part_coef, tile, precision=lax.Precision.HIGHEST, preferred_element_type=jnp.float32
        )

    correction = lax.fori_loop(0, count // width, one_step, empty)
    return field + correction


def solution(mesh):
    in_specs = (
        P("obs", "leaf"),
        P("leaf", None),
        P(None, None, "leaf"),
        P(None, "leaf"),
        P("leaf"),
        P("leaf"),
        P("leaf"),
        P(("leaf", "obs"), None),
    )
    out_specs = P("obs", "leaf")
    return jax.shard_map(body, mesh=mesh, in_specs=in_specs, out_specs=out_specs, check_vma=False)
```

profile of v0, /device:TPU:0, one launch (start us, length us, event | category | flops | bytes accessed | tf_op | source)
XLA Modules:
  0.0 155.6 jit_solution(8411053804030688)
XLA Ops:
  0.0 0.0 copy-start
  0.0 0.0 copy-start.7
  0.0 0.7 copy-done.7
  0.7 0.6 dynamic-slice
  1.9 0.8 dynamic-update-slice
  2.7 13.1 %all-reduce = s32[8]{0:T(128)S(1)} all-reduce(s32[8]{0:T(128)S(1)} %dynamic-update-slice), channel_id=1, replica_groups=mesh['leaf'=8,'obs'=4] {'leaf'}, use_global_device_ids=true, to_apply=%add | all-reduce | flops 8 | bytes 64
  15.8 0.2 reduce-window.8
  15.9 0.1 convert_reduce_fusion
  16.1 0.0 copy-start.3
  16.1 0.1 fusion.23
  16.2 0.6 copy-done.3
  16.8 1.0 fusion.20
  17.8 30.9 %all-gather = f32[128,3,64]{2,0,1:T(8,128)S(1)} all-gather(f32[16,3,64]{2,0,1:T(8,128)S(1)} %fusion.20), channel_id=2, replica_groups=mesh['leaf'=8,'obs'=4] {'leaf'}, dimensions={0}, use_global_device_ids=true | all-gather | bytes 110592 | tf_op jit(solution)/shard_map/all_gather | solution.py:41
  48.6 0.3 fusion.15
  48.9 0.0 copy-start.1
  48.9 0.0 copy-done
  48.9 0.1 fusion.26
  49.1 0.7 copy-done.1
  49.8 0.2 fusion
  50.0 0.0 copy-start.6
  50.1 0.1 copy.17
  50.2 0.6 copy-done.6
  50.8 0.0 copy-start.5
  50.8 0.6 gather_fusion
  51.4 0.0 copy-done.5
  51.4 0.1 subtract_bitcast_fusion
  51.5 31.2 %all_gather.19 = f32[16,1024]{0,1:T(8,128)S(1)} all-gather(f32[16,128]{0,1:T(8,128)S(1)} %subtract_bitcast_fusion), channel_id=1, replica_groups=mesh['leaf'=8,'obs'=4] {'leaf'}, dimensions={1}, use_global_device_ids=true | all-gather | bytes 73728 | tf_op jit(solution)/shard_map/all_gather | solution.py:60
  82.7 0.0 copy-start.2
  82.7 1.0 gather_fusion.1
  83.8 0.0 copy-done.2
  83.8 5.4 %all_gather.21 = f32[64,512]{1,0:T(8,128)S(1)} all-gather(f32[16,512]{1,0:T(8,128)S(1)} %copy-done.2), channel_id=1, replica_groups=mesh['leaf'=8,'obs'=4] {'obs'}, dimensions={0}, use_global_device_ids=true | all-gather | bytes 163840 | tf_op jit(solution)/shard_map/all_gather | solution.py:67
  89.2 0.5 convolution_bitcast_fusion.1
  89.7 30.5 %all-gather.2 = f32[8,64,16]{1,2,0:T(8,128)S(1)} all-gather(f32[1,64,16]{1,2,0:T(8,128)S(1)} %convolution_bitcast_fusion.1), channel_id=1, replica_groups=mesh['leaf'=8,'obs'=4] {'leaf'}, dimensions={0}, use_global_device_ids=true | all-gather | bytes 36864 | tf_op jit(solution)/shard_map/all_gather | solution.py:76
  120.3 0.0 copy-start.4
  120.3 0.1 reshape.123
  120.4 0.6 copy-done.4
  120.9 0.1 copy.19
  121.1 0.6 gather_fusion.2
  121.7 31.3 %all-gather.1 = f32[2,1024]{0,1:T(8,128)S(1)} all-gather(f32[2,128]{0,1:T(8,128)S(1)} %bitcast.43), channel_id=3, replica_groups=mesh['leaf'=8,'obs'=4] {'leaf'}, dimensions={1}, use_global_device_ids=true | all-gather | bytes 9216 | tf_op jit(solution)/shard_map/all_gather | solution.py:61
  153.0 1.0 gather_fusion.3
  154.1 0.3 slice_reduce_fusion.1
  154.4 1.3 convolution_add_fusion
  (10 shorter events, 0.1 us)
Async XLA Ops:
  0.0 48.9 %copy-start = (bf16[256,256]{1,0:T(8,128)(2,1)S(1)}, bf16[256,256]{1,0:T(8,128)(2,1)}, u32[]{:S(2)}) copy-start(bf16[256,256]{1,0:T(8,128)(2,1)} %param.9) | copy-start | bytes 393220
  0.0 0.7 copy-start.7
  16.1 0.7 copy-start.3
  48.9 0.9 copy-start.1
  50.0 0.7 copy-start.6
  50.8 0.7 copy-start.5
  82.7 1.0 copy-start.2
  120.3 0.7 copy-start.4
where the time goes:
time: 156 us
  blocking collectives  142 us (91%)
  local copies, waits for them, and re-layouts  8.54 us (5%)
  matrix products  3.48 us (2%)
    all_gather x1, blocking collectives, body(): lax.all_gather(local_xy, 'leaf', axis=1, tiled=True)  31.3 us
    all_gather x1, blocking collectives, body(): lax.all_gather(residual, 'leaf', axis=1, tiled=True)  31.2 us
    all_gather x1, blocking collectives, body(): everyone = lax.all_gather(project[None], 'leaf', axis=0, tiled=True)  30.9 us
    all_gather x1, blocking collectives, body(): piece = lax.all_gather(fold_coef, 'leaf', axis=1, tiled=True)  30.5 us
    unnamed x1, blocking collectives  13.1 us
    all_gather x1, blocking collectives, body(): block_rows = lax.all_gather(inverse_rows, 'obs', axis=0, tiled=True)  5.43 us
    unnamed x21, local copies, waits for them, and re-layouts  4.75 us

commit v1 on v0

v1 whole, which is shorter than its diff:
```python
import functools

import jax
import jax.numpy as jnp
from jax import lax
from jax.experimental import pallas as pl
from jax.experimental.pallas import tpu as pltpu
from jax.sharding import PartitionSpec as P

corr_length = 0.15
MESH = pl.DeviceIdType.MESH
NT = (((1,), (1,)), ((), ()))
UNROLL = 8
CHUNK = 512
MSG = 16


def dot(a, b):
    return jnp.dot(a, b, preferred_element_type=jnp.float32)


def dot_nt(a, b):
    return lax.dot_general(a, b, NT, preferred_element_type=jnp.float32)


def split(a):
    high = a.astype(jnp.bfloat16)
    return high, (a - high.astype(jnp.float32)).astype(jnp.bfloat16)


def stacked(a):
    high, low = split(a)
    return jnp.concatenate([high, low], axis=0)


def loop(count, step):
    if count <= UNROLL:
        for i in range(count):
            step(i)
    else:

        def one(i, carry):
            step(i)
            return carry

        lax.fori_loop(0, count, one, 0)


def at(start, size):
    start = start if isinstance(start, int) else pl.multiple_of(start, size)
    return pl.ds(start, size)


def kernel(
    leaves,
    groups,
    z_ref,
    diag_ref,
    basis_ref,
    xy_ref,
    site_ref,
    value_ref,
    count_ref,
    inv_ref,
    out_ref,
    proj,
    abuf,
    mbuf,
    ibuf,
    rbuf,
    cbuf,
    xbuf,
    sbuf,
    kh,
    kl,
    slot_of,
    a_send,
    a_recv,
    m_send,
    m_recv,
    i_send,
    i_recv,
    r_send,
    r_recv,
    c_send,
    c_recv,
):
    p = lax.axis_index("leaf")
    o = lax.axis_index("obs")
    levels, rank, sites = basis_ref.shape
    samples = z_ref.shape[0]
    slots = site_ref.shape[1]
    rows = inv_ref.shape[0]
    total = inv_ref.shape[1]
    owned = rows * groups

    def partners(step):
        for level in reversed(range(levels)):
            width = 2**level
            half = p // width
            start = (half + 1 - 2 * (half % 2)) * width
            loop(width, functools.partial(lambda level, start, i: step(level, start + i), level, start))

    def peers(step):
        for e in range(1, groups):
            step((o + e) % groups)

    barrier = pltpu.get_barrier_semaphore()

    def greet(leaf, obs):
        pl.semaphore_signal(barrier, inc=1, device_id=(leaf, obs), device_id_type=MESH)

    partners(lambda level, q: greet(q, o))
    peers(lambda g: greet(p, g))

    def to_leaf(src, dst, send, recv, q, who):
        return pltpu.make_async_remote_copy(
            src_ref=src, dst_ref=dst, send_sem=send.at[q], recv_sem=recv.at[who],
            device_id=(q, o), device_id_type=MESH,
        )

    def a_copy(level, q, who):
        return to_leaf(proj.at[level], abuf.at[who], a_send, a_recv, q, who)

    def m_copy(q, who):
        return to_leaf(mbuf.at[who], mbuf.at[who], m_send, m_recv, q, who)

    def r_copy(q, who):
        part = rbuf.at[:, at(who * slots, slots)]
        return to_leaf(part, part, r_send, r_recv, q, who)

    def c_copy(q, who):
        return to_leaf(cbuf.at[who], cbuf.at[who], c_send, c_recv, q, who)

    def i_copy(g, who):
        part = ibuf.at[at(who * rows, rows), :]
        return pltpu.make_async_remote_copy(
            src_ref=part, dst_ref=part, send_sem=i_send.at[g], recv_sem=i_recv.at[who],
            device_id=(p, g), device_id_type=MESH,
        )

    z = z_ref[...]
    for level in range(levels):
        proj[level] = dot_nt(z, basis_ref[level])
    pick = (lax.broadcasted_iota(jnp.int32, (sites, slots), 0) == site_ref[...]).astype(jnp.float32)
    pick = pick.astype(jnp.bfloat16)
    row = lax.broadcasted_iota(jnp.int32, (MSG, sites), 0)
    coord = jnp.where(row < 3, xy_ref[0:1, :], xy_ref[1:2, :])
    first = coord.astype(jnp.bfloat16).astype(jnp.float32)
    second = (coord - first).astype(jnp.bfloat16).astype(jnp.float32)
    third = coord - first - second
    part = jnp.where(row % 3 == 0, first, jnp.where(row % 3 == 1, second, third))
    part = jnp.where(row < 6, part, 0.0).astype(jnp.bfloat16)
    message = dot(part, pick)
    count = count_ref[0].astype(jnp.float32)
    message = jnp.where(lax.broadcasted_iota(jnp.int32, (MSG, slots), 0) == 6, count, message)
    mbuf[p] = message
    ibuf[at(o * rows, rows), :] = inv_ref[...]

    pl.semaphore_wait(barrier, leaves - 1 + groups - 1)

    partners(lambda level, q: a_copy(level, q, p).start())
    partners(lambda level, q: m_copy(q, p).start())
    peers(lambda g: i_copy(g, o).start())

    at_slots = value_ref[...] - dot(z, dot(diag_ref[...], pick).astype(jnp.bfloat16))
    picked = [dot(basis_ref[level], pick).astype(jnp.bfloat16) for level in range(levels)]
    field = dot(z, diag_ref[...])

    partners(lambda level, q: a_copy(level, q, q).wait_recv())
    coefs = []
    for level in range(levels):
        width = 2**level
        half = p // width
        start = (half + 1 - 2 * (half % 2)) * width
        sums = abuf[start]
        if width <= UNROLL:
            for i in range(1, width):
                sums = sums + abuf[start + i]
        else:
            sums = lax.fori_loop(1, width, lambda i, s, start=start: s + abuf[start + i], sums)
        coefs.append(stacked(sums * (0.5 / (rank * width * sites) ** 0.5)))
    low = dot(coefs[0], picked[0])
    for level in range(1, levels):
        low = low + dot(coefs[level], picked[level])
    rbuf[:, at(p * slots, slots)] = at_slots - (low[:samples] + low[samples:])
    partners(lambda level, q: r_copy(q, p).start())

    low = dot(coefs[0], basis_ref[0])
    for level in range(1, levels):
        low = low + dot(coefs[level], basis_ref[level])
    out_ref[...] = field + (low[:samples] + low[samples:])

    partners(lambda level, q: m_copy(q, q).wait_recv())
    counts = jnp.concatenate([mbuf[q, 6:7, :] for q in range(leaves)], axis=0)
    below = lax.broadcasted_iota(jnp.int32, (leaves, leaves), 1) < lax.broadcasted_iota(
        jnp.int32, (leaves, leaves), 0
    )
    base = dot(below.astype(jnp.float32).astype(jnp.bfloat16), counts.astype(jnp.bfloat16))
    lane = lax.broadcasted_iota(jnp.int32, (leaves, slots), 1).astype(jnp.float32)
    slot_of[...] = jnp.where(lane < counts, base + lane, -1.0)
    chunk = min(CHUNK, total)
    number = lax.broadcasted_iota(jnp.int32, (chunk, slots), 0).astype(jnp.float32)
    peers(lambda g: i_copy(g, g).wait_recv())

    def one_chunk(c):
        inverse = stacked(ibuf[:, at(c * chunk, chunk)])
        shift = number + jnp.float32(c * chunk) if isinstance(c, int) else number + (c * chunk).astype(jnp.float32)

        def one_leaf(q):
            here = jnp.where(shift == slot_of[pl.ds(q, 1), :], 1.0, 0.0).astype(jnp.bfloat16)
            wide = dot(inverse, here)
            wide = wide[:owned] + wide[owned:]
            lanes = at(q * slots, slots)
            if chunk == total:
                xbuf[:, lanes] = wide
            else:
                xbuf[:, lanes] += wide
            places = dot_nt(here, mbuf[q].astype(jnp.bfloat16))
            if isinstance(q, int) and q == 0:
                sbuf[...] = places
            else:
                sbuf[...] += places

        if leaves > UNROLL:
            sbuf[...] = jnp.zeros_like(sbuf)
        loop(leaves, one_leaf)
        places = sbuf[...]

        def column(i):
            return jnp.broadcast_to(places[:, i : i + 1], (chunk, sites))

        delta_x = (column(0) + column(1) + column(2)) - xy_ref[0:1, :]
        delta_y = (column(3) + column(4) + column(5)) - xy_ref[1:2, :]
        distance = jnp.sqrt(delta_x * delta_x + delta_y * delta_y)
        high, rest = split(jnp.exp(distance * (-1.0 / corr_length)))
        kh[at(c * chunk, chunk), :] = high
        kl[at(c * chunk, chunk), :] = rest

    if chunk < total:
        xbuf[...] = jnp.zeros_like(xbuf)
    loop(total // chunk, one_chunk)
    xh, xl = split(xbuf[...])

    partners(lambda level, q: r_copy(q, q).wait_recv())
    rh, rl = split(rbuf[...])
    both = dot_nt(jnp.concatenate([rh, rl], axis=0), xh)
    cbuf[p] = both[:samples] + both[samples:] + dot_nt(rh, xl)
    partners(lambda level, q: c_copy(q, p).start())

    def drain(level, q):
        a_copy(level, q, p).wait_send()
        m_copy(q, p).wait_send()
        r_copy(q, p).wait_send()

    partners(drain)
    peers(lambda g: i_copy(g, o).wait_send())
    partners(lambda level, q: c_copy(q, q).wait_recv())

    def correct(q):
        coef = stacked(cbuf[q])
        lines = at(q * owned, owned)
        twice = dot(coef, kh[lines, :])
        return twice[:samples] + twice[samples:] + dot(coef[:samples], kl[lines, :])

    if leaves <= UNROLL:
        total_sum = correct(0)
        for q in range(1, leaves):
            total_sum = total_sum + correct(q)
    else:
        total_sum = lax.fori_loop(1, leaves, lambda q, s: s + correct(q), correct(0))
    out_ref[...] += total_sum
    partners(lambda level, q: c_copy(q, p).wait_send())


def body(samples_z, diag_block, level_basis, site_xy, obs_site, obs_value, obs_count, inverse_rows):
    leaves = lax.axis_size("leaf")
    groups = lax.axis_size("obs")
    samples, sites = samples_z.shape
    levels, rank, _ = level_basis.shape
    slots = obs_site.shape[0]
    rows, total = inverse_rows.shape
    owned = rows * groups
    vmem = pl.BlockSpec(memory_space=pltpu.VMEM)
    smem = pl.BlockSpec(memory_space=pltpu.SMEM)
    f32, bf16 = jnp.float32, jnp.bfloat16
    leaf_sem = pltpu.SemaphoreType.DMA((leaves,))
    obs_sem = pltpu.SemaphoreType.DMA((groups,))
    return pl.pallas_call(
        functools.partial(kernel, leaves, groups),
        out_shape=jax.ShapeDtypeStruct((samples, sites), f32),
        in_specs=[vmem] * 6 + [smem, vmem],
        out_specs=vmem,
        scratch_shapes=[
            pltpu.VMEM((levels, samples, rank), f32),
            pltpu.VMEM((leaves, samples, rank), f32),
            pltpu.VMEM((leaves, MSG, slots), f32),
            pltpu.VMEM((owned, total), f32),
            pltpu.VMEM((samples, leaves * slots), f32),
            pltpu.VMEM((leaves, samples, owned), f32),
            pltpu.VMEM((owned, leaves * slots), f32),
            pltpu.VMEM((min(CHUNK, total), MSG), f32),
            pltpu.VMEM((total, sites), bf16),
            pltpu.VMEM((total, sites), bf16),
            pltpu.VMEM((leaves, slots), f32),
            leaf_sem, leaf_sem, leaf_sem, leaf_sem,
            obs_sem, obs_sem,
            leaf_sem, leaf_sem, leaf_sem, leaf_sem,
        ],
        compiler_params=pltpu.CompilerParams(
            collective_id=0, has_side_effects=True, vmem_limit_bytes=40 * 2**20
        ),
        cost_estimate=pl.CostEstimate(
            flops=2 * samples * sites * total * 4,
            bytes_accessed=4 * owned * total,
            transcendentals=2 * total * sites,
        ),
    )(
        samples_z,
        diag_block,
        level_basis,
        site_xy,
        obs_site.reshape(1, slots),
        obs_value.reshape(1, slots),
        obs_count,
        inverse_rows,
    )


def solution(mesh):
    in_specs = (
        P("obs", "leaf"),
        P("leaf", None),
        P(None, None, "leaf"),
        P(None, "leaf"),
        P("leaf"),
        P("leaf"),
        P("leaf"),
        P(("leaf", "obs"), None),
    )
    out_specs = P("obs", "leaf")
    return jax.shard_map(body, mesh=mesh, in_specs=in_specs, out_specs=out_specs, check_vma=False)
```

time: 156 us -> 24.2 us (0.16)
  blocking collectives: 142 us -> 0 us
  Pallas kernels: 0 us -> 18.7 us
  local copies, waits for them, and re-layouts: 8.54 us -> 4.52 us
  matrix products: 3.48 us -> 0 us
    all_gather x5 -> x0, blocking collectives: 129 us -> none  [the longest x1 31.3 us: body(): lax.all_gather(local_xy, 'leaf', axis=1, tiled=True)]
    pallas_call x0 -> x1, Pallas kernels: none -> 18.7 us  [body(): pl.pallas_call(functools.partial(kernel, leaves, groups), out_shape=jax.S...]
    unnamed x1 -> x0, blocking collectives: 13.1 us -> none
    dot_general x6 -> x0, matrix products: 3.48 us -> none  [the longest x1 1.26 us: one_step(): jnp.dot(part_coef, tile, precision=lax.Precision.HIGHEST, preferred_eleme...]
    gather x4 -> x0, local copies, waits for them, and re-layouts: 3.35 us -> none  [the longest x1 1.03 us: body(): resid_comp = resid_all[:, obs_index]]
    unnamed x21 -> x15, local copies, waits for them, and re-layouts: 4.75 us -> 4.52 us
where the time goes in v1:
time: 24.2 us; the launch traced here: 23.9 us
  Pallas kernels  18.7 us (77%)
  local copies, waits for them, and re-layouts  4.52 us (19%)
  between operations  0.69 us (3%)
    pallas_call x1, Pallas kernels, body(): pl.pallas_call(functools.partial(kernel, leaves, groups), out_shape=jax.S...  18.7 us
    unnamed x15, local copies, waits for them, and re-layouts  4.52 us

profile of v1, /device:TPU:0, one launch (start us, length us, event | category | flops | bytes accessed | tf_op | source)
XLA Modules:
  0.0 23.9 jit_solution(17125251935689467224)
XLA Ops:
  0.7 0.0 copy-start.4
  0.7 0.0 copy-start.5
  0.7 0.0 copy-start.6
  0.7 0.7 %copy-done.4 = f32[2,256]{1,0:T(2,128)S(1)} copy-done((f32[2,256]{1,0:T(2,128)S(1)}, f32[2,256]{1,0:T(2,128)}, u32[]{:S(2)}) %copy-start.4) | copy-done | bytes 2072
  1.3 0.0 copy-done.5
  1.3 0.0 copy-done.6
  1.3 0.0 copy-start
  1.3 0.9 %copy-done = bf16[256,256]{1,0:T(8,128)(2,1)S(1)} copy-done((bf16[256,256]{1,0:T(8,128)(2,1)S(1)}, bf16[256,256]{1,0:T(8,128)(2,1)}, u32[]{:S(2)}) %copy-start) | copy-done | bytes 131096
  2.2 0.0 copy-start.1
  2.2 0.9 %copy-done.1 = bf16[3,64,256]{2,1,0:T(8,128)(2,1)S(1)} copy-done((bf16[3,64,256]{2,1,0:T(8,128)(2,1)S(1)}, bf16[3,64,256]{2,1,0:T(8,128)(2,1)}, u32[]{:S(2)}) %copy-start.1) | copy-done | bytes 98328
  3.1 0.0 copy-start.2
  3.1 0.8 %copy-done.2 = f32[16,512]{1,0:T(8,128)S(1)} copy-done((f32[16,512]{1,0:T(8,128)S(1)}, f32[16,512]{1,0:T(8,128)}, u32[]{:S(2)}) %copy-start.2) | copy-done | bytes 32792
  3.9 0.0 copy-start.3
  3.9 0.7 %copy-done.3 = bf16[16,256]{1,0:T(8,128)(2,1)S(1)} copy-done((bf16[16,256]{1,0:T(8,128)(2,1)S(1)}, bf16[16,256]{1,0:T(8,128)(2,1)}, u32[]{:S(2)}) %copy-start.3) | copy-done | bytes 8216
  4.6 18.7 %shard_map.82 = f32[16,256]{1,0:T(8,128)S(1)} custom-call(bf16[16,256]{1,0:T(8,128)(2,1)S(1)} %copy-done.3, bf16[256,256]{1,0:T(8,128)(2,1)S(1)} %copy-done, bf16[3,64,256]{2,1,0:T(8,128)(2,1)S(1)} %copy-done.1, f32[2,256]{1,0:T(2,128)S(1)} %copy-done.4, s32[1,128]{1,0:T(1,128)S(1)} %bitcast.2, f32[1,128]{1,0:T(1,128)S(1)} %bitcast.3, s32[1]{0:T(128)S(6)} %copy.10.count_ref, ...), custom_call_target="tpu_custom_call" | custom-call | flops 16777216 | bytes 131072 | tf_op jit(solution)/shard_map/pallas_call | solution.py:289
  23.3 0.6 %copy.11 = f32[16,256]{1,0:T(8,128)} copy(f32[16,256]{1,0:T(8,128)S(1)} %shard_map.82) | data formatting | bytes 32768
Async XLA Ops:
  0.7 0.7 %copy-start.4 = (f32[2,256]{1,0:T(2,128)S(1)}, f32[2,256]{1,0:T(2,128)}, u32[]{:S(2)}) copy-start(f32[2,256]{1,0:T(2,128)} %xy_ref.1) | copy-start | bytes 6148
  0.7 0.7 %copy-start.5 = (s32[128]{0:T(128)S(1)}, s32[128]{0:T(128)}, u32[]{:S(2)}) copy-start(s32[128]{0:T(128)} %param.12) | copy-start | bytes 1540
  0.7 0.7 %copy-start.6 = (f32[128]{0:T(128)S(1)}, f32[128]{0:T(128)}, u32[]{:S(2)}) copy-start(f32[128]{0:T(128)} %param.13) | copy-start | bytes 1540
  1.3 0.9 %copy-start = (bf16[256,256]{1,0:T(8,128)(2,1)S(1)}, bf16[256,256]{1,0:T(8,128)(2,1)}, u32[]{:S(2)}) copy-start(bf16[256,256]{1,0:T(8,128)(2,1)} %diag_ref.1) | copy-start | bytes 393220
  2.2 0.9 %copy-start.1 = (bf16[3,64,256]{2,1,0:T(8,128)(2,1)S(1)}, bf16[3,64,256]{2,1,0:T(8,128)(2,1)}, u32[]{:S(2)}) copy-start(bf16[3,64,256]{2,1,0:T(8,128)(2,1)} %basis_ref.1) | copy-start | bytes 294916
  3.1 0.8 %copy-start.2 = (f32[16,512]{1,0:T(8,128)S(1)}, f32[16,512]{1,0:T(8,128)}, u32[]{:S(2)}) copy-start(f32[16,512]{1,0:T(8,128)} %inv_ref.1) | copy-start | bytes 98308
  3.9 0.7 %copy-start.3 = (bf16[16,256]{1,0:T(8,128)(2,1)S(1)}, bf16[16,256]{1,0:T(8,128)(2,1)}, u32[]{:S(2)}) copy-start(bf16[16,256]{1,0:T(8,128)(2,1)} %z_ref.1) | copy-start | bytes 24580

commit v2 on v1

--- a/solution.py
+++ b/solution.py
@@ -54,6 +54,15 @@
 def kernel(
     leaves,
     groups,
+    z_hbm,
+    diag_hbm,
+    basis_hbm,
+    xy_hbm,
+    site_hbm,
+    value_hbm,
+    count_hbm,
+    inv_hbm,
+    out_ref,
     z_ref,
     diag_ref,
     basis_ref,
@@ -61,8 +70,7 @@
     site_ref,
     value_ref,
     count_ref,
-    inv_ref,
-    out_ref,
+    in_sem,
     proj,
     abuf,
     mbuf,
@@ -90,8 +98,7 @@
     levels, rank, sites = basis_ref.shape
     samples = z_ref.shape[0]
     slots = site_ref.shape[1]
-    rows = inv_ref.shape[0]
-    total = inv_ref.shape[1]
+    rows, total = inv_hbm.shape
     owned = rows * groups
 
     def partners(step):
@@ -105,6 +112,14 @@
         for e in range(1, groups):
             step((o + e) % groups)
 
+    own_rows = ibuf.at[at(o * rows, rows), :]
+    moves = [
+        (z_hbm, z_ref), (basis_hbm, basis_ref), (site_hbm, site_ref), (xy_hbm, xy_ref),
+        (count_hbm, count_ref), (diag_hbm, diag_ref), (value_hbm, value_ref), (inv_hbm, own_rows),
+    ]
+    loads = [pltpu.make_async_copy(src, dst, in_sem.at[i]) for i, (src, dst) in enumerate(moves)]
+    for load in loads:
+        load.start()
     barrier = pltpu.get_barrier_semaphore()
 
     def greet(leaf, obs):
@@ -135,13 +150,22 @@
     def i_copy(g, who):
         part = ibuf.at[at(who * rows, rows), :]
         return pltpu.make_async_remote_copy(
-            src_ref=part, dst_ref=part, send_sem=i_send.at[g], recv_sem=i_recv.at[who],
+            src_ref=inv_hbm, dst_ref=part, send_sem=i_send.at[g], recv_sem=i_recv.at[who],
             device_id=(p, g), device_id_type=MESH,
         )
 
+    loads[0].wait()
+    loads[1].wait()
     z = z_ref[...]
     for level in range(levels):
         proj[level] = dot_nt(z, basis_ref[level])
+
+    pl.semaphore_wait(barrier, leaves - 1 + groups - 1)
+    partners(lambda level, q: a_copy(level, q, p).start())
+    peers(lambda g: i_copy(g, o).start())
+
+    for load in loads[2:5]:
+        load.wait()
     pick = (lax.broadcasted_iota(jnp.int32, (sites, slots), 0) == site_ref[...]).astype(jnp.float32)
     pick = pick.astype(jnp.bfloat16)
     row = lax.broadcasted_iota(jnp.int32, (MSG, sites), 0)
@@ -155,14 +179,9 @@
     count = count_ref[0].astype(jnp.float32)
     message = jnp.where(lax.broadcasted_iota(jnp.int32, (MSG, slots), 0) == 6, count, message)
     mbuf[p] = message
-    ibuf[at(o * rows, rows), :] = inv_ref[...]
-
-    pl.semaphore_wait(barrier, leaves - 1 + groups - 1)
-
-    partners(lambda level, q: a_copy(level, q, p).start())
     partners(lambda level, q: m_copy(q, p).start())
-    peers(lambda g: i_copy(g, o).start())
-
+    for load in loads[5:]:
+        load.wait()
     at_slots = value_ref[...] - dot(z, dot(diag_ref[...], pick).astype(jnp.bfloat16))
     picked = [dot(basis_ref[level], pick).astype(jnp.bfloat16) for level in range(levels)]
     field = dot(z, diag_ref[...])
@@ -186,11 +205,6 @@
     rbuf[:, at(p * slots, slots)] = at_slots - (low[:samples] + low[samples:])
     partners(lambda level, q: r_copy(q, p).start())
 
-    low = dot(coefs[0], basis_ref[0])
-    for level in range(1, levels):
-        low = low + dot(coefs[level], basis_ref[level])
-    out_ref[...] = field + (low[:samples] + low[samples:])
-
     partners(lambda level, q: m_copy(q, q).wait_recv())
     counts = jnp.concatenate([mbuf[q, 6:7, :] for q in range(leaves)], axis=0)
     below = lax.broadcasted_iota(jnp.int32, (leaves, leaves), 1) < lax.broadcasted_iota(
@@ -217,26 +231,16 @@
             else:
                 xbuf[:, lanes] += wide
             places = dot_nt(here, mbuf[q].astype(jnp.bfloat16))
+            lines = at(c * chunk, chunk)
             if isinstance(q, int) and q == 0:
-                sbuf[...] = places
+                sbuf[lines, :] = places
             else:
-                sbuf[...] += places
-
-        if leaves > UNROLL:
-            sbuf[...] = jnp.zeros_like(sbuf)
+                sbuf[lines, :] += places
+
         loop(leaves, one_leaf)
-        places = sbuf[...]
-
-        def column(i):
-            return jnp.broadcast_to(places[:, i : i + 1], (chunk, sites))
-
-        delta_x = (column(0) + column(1) + column(2)) - xy_ref[0:1, :]
-        delta_y = (column(3) + column(4) + column(5)) - xy_ref[1:2, :]
-        distance = jnp.sqrt(delta_x * delta_x + delta_y * delta_y)
-        high, rest = split(jnp.exp(distance * (-1.0 / corr_length)))
-        kh[at(c * chunk, chunk), :] = high
-        kl[at(c * chunk, chunk), :] = rest
-
+
+    if leaves > UNROLL:
+        sbuf[...] = jnp.zeros_like(sbuf)
     if chunk < total:
         xbuf[...] = jnp.zeros_like(xbuf)
     loop(total // chunk, one_chunk)
@@ -247,6 +251,25 @@
     both = dot_nt(jnp.concatenate([rh, rl], axis=0), xh)
     cbuf[p] = both[:samples] + both[samples:] + dot_nt(rh, xl)
     partners(lambda level, q: c_copy(q, p).start())
+
+    low = dot(coefs[0], basis_ref[0])
+    for level in range(1, levels):
+        low = low + dot(coefs[level], basis_ref[level])
+    out_ref[...] = field + (low[:samples] + low[samples:])
+
+    def one_tile(c):
+        lines = at(c * chunk, chunk)
+        places = sbuf[lines, :]
+
+        def column(i):
+            return jnp.broadcast_to(places[:, i : i + 1], (chunk, sites))
+
+        delta_x = (column(0) + column(1) + column(2)) - xy_ref[0:1, :]
+        delta_y = (column(3) + column(4) + column(5)) - xy_ref[1:2, :]
+        distance = jnp.sqrt(delta_x * delta_x + delta_y * delta_y)
+        kh[lines, :], kl[lines, :] = split(jnp.exp(distance * (-1.0 / corr_length)))
+
+    loop(total // chunk, one_tile)
 
     def drain(level, q):
         a_copy(level, q, p).wait_send()
@@ -282,16 +305,24 @@
     rows, total = inverse_rows.shape
     owned = rows * groups
     vmem = pl.BlockSpec(memory_space=pltpu.VMEM)
-    smem = pl.BlockSpec(memory_space=pltpu.SMEM)
+    hbm = pl.BlockSpec(memory_space=pltpu.HBM)
     f32, bf16 = jnp.float32, jnp.bfloat16
     leaf_sem = pltpu.SemaphoreType.DMA((leaves,))
     obs_sem = pltpu.SemaphoreType.DMA((groups,))
     return pl.pallas_call(
         functools.partial(kernel, leaves, groups),
         out_shape=jax.ShapeDtypeStruct((samples, sites), f32),
-        in_specs=[vmem] * 6 + [smem, vmem],
+        in_specs=[hbm] * 8,
         out_specs=vmem,
         scratch_shapes=[
+            pltpu.VMEM(samples_z.shape, bf16),
+            pltpu.VMEM(diag_block.shape, bf16),
+            pltpu.VMEM(level_basis.shape, bf16),
+            pltpu.VMEM(site_xy.shape, f32),
+            pltpu.VMEM((1, slots), jnp.int32),
+            pltpu.VMEM((1, slots), f32),
+            pltpu.SMEM((1,), jnp.int32),
+            pltpu.SemaphoreType.DMA((8,)),
             pltpu.VMEM((levels, samples, rank), f32),
             pltpu.VMEM((leaves, samples, rank), f32),
             pltpu.VMEM((leaves, MSG, slots), f32),
@@ -299,7 +330,7 @@
             pltpu.VMEM((samples, leaves * slots), f32),
             pltpu.VMEM((leaves, samples, owned), f32),
             pltpu.VMEM((owned, leaves * slots), f32),
-            pltpu.VMEM((min(CHUNK, total), MSG), f32),
+            pltpu.VMEM((total, MSG), f32),
             pltpu.VMEM((total, sites), bf16),
             pltpu.VMEM((total, sites), bf16),
             pltpu.VMEM((leaves, slots), f32),

time: 24.2 us -> 24.7 us (1.021)
  Pallas kernels: 18.7 us -> 19.2 us
    pallas_call x1, Pallas kernels: 18.7 us -> 19.2 us  [body(): pl.pallas_call(functools.partial(kernel, leaves, groups), out_shape=jax.S...]
where the time goes in v2:
time: 24.7 us; the launch traced here: 24.4 us
  Pallas kernels  19.2 us (78%)
  local copies, waits for them, and re-layouts  4.52 us (18%)
  between operations  0.69 us (3%)
    pallas_call x1, Pallas kernels, body(): pl.pallas_call(functools.partial(kernel, leaves, groups), out_shape=jax.S...  19.2 us
    unnamed x15, local copies, waits for them, and re-layouts  4.52 us

profile of v2, /device:TPU:0, one launch (start us, length us, event | category | flops | bytes accessed | tf_op | source)
XLA Modules:
  0.0 24.4 jit_solution(17784774231960859724)
XLA Ops:
  0.7 0.0 copy-start.4
  0.7 0.0 copy-start.5
  0.7 0.0 copy-start.6
  0.7 0.7 %copy-done.4 = f32[2,256]{1,0:T(2,128)S(1)} copy-done((f32[2,256]{1,0:T(2,128)S(1)}, f32[2,256]{1,0:T(2,128)}, u32[]{:S(2)}) %copy-start.4) | copy-done | bytes 2072
  1.3 0.0 copy-done.5
  1.3 0.0 copy-done.6
  1.3 0.0 copy-start
  1.3 0.9 %copy-done = bf16[256,256]{1,0:T(8,128)(2,1)S(1)} copy-done((bf16[256,256]{1,0:T(8,128)(2,1)S(1)}, bf16[256,256]{1,0:T(8,128)(2,1)}, u32[]{:S(2)}) %copy-start) | copy-done | bytes 131096
  2.2 0.0 copy-start.1
  2.2 0.9 %copy-done.1 = bf16[3,64,256]{2,1,0:T(8,128)(2,1)S(1)} copy-done((bf16[3,64,256]{2,1,0:T(8,128)(2,1)S(1)}, bf16[3,64,256]{2,1,0:T(8,128)(2,1)}, u32[]{:S(2)}) %copy-start.1) | copy-done | bytes 98328
  3.1 0.0 copy-start.2
  3.1 0.8 %copy-done.2 = f32[16,512]{1,0:T(8,128)S(1)} copy-done((f32[16,512]{1,0:T(8,128)S(1)}, f32[16,512]{1,0:T(8,128)}, u32[]{:S(2)}) %copy-start.2) | copy-done | bytes 32792
  3.9 0.0 copy-start.3
  3.9 0.7 %copy-done.3 = bf16[16,256]{1,0:T(8,128)(2,1)S(1)} copy-done((bf16[16,256]{1,0:T(8,128)(2,1)S(1)}, bf16[16,256]{1,0:T(8,128)(2,1)}, u32[]{:S(2)}) %copy-start.3) | copy-done | bytes 8216
  4.6 19.2 %shard_map.82 = f32[16,256]{1,0:T(8,128)S(1)} custom-call(bf16[16,256]{1,0:T(8,128)(2,1)S(1)} %copy-done.3, bf16[256,256]{1,0:T(8,128)(2,1)S(1)} %copy-done, bf16[3,64,256]{2,1,0:T(8,128)(2,1)S(1)} %copy-done.1, f32[2,256]{1,0:T(2,128)S(1)} %copy-done.4, s32[1,128]{1,0:T(1,128)S(1)} %bitcast.2, f32[1,128]{1,0:T(1,128)S(1)} %bitcast.3, s32[1]{0:T(128)S(6)} %copy.10.count_hbm, ...), custom_call_target="tpu_custom_call" | custom-call | flops 16777216 | bytes 131072 | tf_op jit(solution)/shard_map/pallas_call | solution.py:312
  23.8 0.6 %copy.11 = f32[16,256]{1,0:T(8,128)} copy(f32[16,256]{1,0:T(8,128)S(1)} %shard_map.82) | data formatting | bytes 32768
Async XLA Ops:
  0.7 0.7 %copy-start.4 = (f32[2,256]{1,0:T(2,128)S(1)}, f32[2,256]{1,0:T(2,128)}, u32[]{:S(2)}) copy-start(f32[2,256]{1,0:T(2,128)} %xy_hbm.1) | copy-start | bytes 6148
  0.7 0.7 %copy-start.5 = (s32[128]{0:T(128)S(1)}, s32[128]{0:T(128)}, u32[]{:S(2)}) copy-start(s32[128]{0:T(128)} %param.12) | copy-start | bytes 1540
  0.7 0.7 %copy-start.6 = (f32[128]{0:T(128)S(1)}, f32[128]{0:T(128)}, u32[]{:S(2)}) copy-start(f32[128]{0:T(128)} %param.13) | copy-start | bytes 1540
  1.3 0.9 %copy-start = (bf16[256,256]{1,0:T(8,128)(2,1)S(1)}, bf16[256,256]{1,0:T(8,128)(2,1)}, u32[]{:S(2)}) copy-start(bf16[256,256]{1,0:T(8,128)(2,1)} %diag_hbm.1) | copy-start | bytes 393220
  2.2 0.9 %copy-start.1 = (bf16[3,64,256]{2,1,0:T(8,128)(2,1)S(1)}, bf16[3,64,256]{2,1,0:T(8,128)(2,1)}, u32[]{:S(2)}) copy-start(bf16[3,64,256]{2,1,0:T(8,128)(2,1)} %basis_hbm.1) | copy-start | bytes 294916
  3.1 0.8 %copy-start.2 = (f32[16,512]{1,0:T(8,128)S(1)}, f32[16,512]{1,0:T(8,128)}, u32[]{:S(2)}) copy-start(f32[16,512]{1,0:T(8,128)} %inv_hbm.1) | copy-start | bytes 98308
  3.9 0.7 %copy-start.3 = (bf16[16,256]{1,0:T(8,128)(2,1)S(1)}, bf16[16,256]{1,0:T(8,128)(2,1)}, u32[]{:S(2)}) copy-start(bf16[16,256]{1,0:T(8,128)(2,1)} %z_hbm.1) | copy-start | bytes 24580

commit v3 on v2

--- a/solution.py
+++ b/solution.py
@@ -78,6 +78,7 @@
     rbuf,
     cbuf,
     xbuf,
+    xt,
     sbuf,
     kh,
     kl,
@@ -100,6 +101,10 @@
     slots = site_ref.shape[1]
     rows, total = inv_hbm.shape
     owned = rows * groups
+    pack = max(1, min(leaves, 128 // owned))
+    depth = levels * rank
+    side = max(1, 128 // rank)
+    tile = side * rank
 
     def partners(step):
         for level in reversed(range(levels)):
@@ -135,7 +140,7 @@
         )
 
     def a_copy(level, q, who):
-        return to_leaf(proj.at[level], abuf.at[who], a_send, a_recv, q, who)
+        return to_leaf(proj.at[level // side], abuf.at[who], a_send, a_recv, q, who)
 
     def m_copy(q, who):
         return to_leaf(mbuf.at[who], mbuf.at[who], m_send, m_recv, q, who)
@@ -157,8 +162,13 @@
     loads[0].wait()
     loads[1].wait()
     z = z_ref[...]
-    for level in range(levels):
-        proj[level] = dot_nt(z, basis_ref[level])
+    basis = basis_ref[...].reshape(depth, sites)
+    project = dot_nt(z, basis)
+    spare = proj.shape[0] * tile - depth
+    if spare:
+        project = jnp.concatenate([project, jnp.zeros((samples, spare), jnp.float32)], axis=1)
+    for i in range(proj.shape[0]):
+        proj[i] = project[:, i * tile : (i + 1) * tile]
 
     pl.semaphore_wait(barrier, leaves - 1 + groups - 1)
     partners(lambda level, q: a_copy(level, q, p).start())
@@ -183,11 +193,12 @@
     for load in loads[5:]:
         load.wait()
     at_slots = value_ref[...] - dot(z, dot(diag_ref[...], pick).astype(jnp.bfloat16))
-    picked = [dot(basis_ref[level], pick).astype(jnp.bfloat16) for level in range(levels)]
+    picked = dot(basis, pick).astype(jnp.bfloat16)
     field = dot(z, diag_ref[...])
 
     partners(lambda level, q: a_copy(level, q, q).wait_recv())
-    coefs = []
+    coefs = [jnp.zeros((samples, tile), jnp.float32)] * proj.shape[0]
+    part_of = lax.broadcasted_iota(jnp.int32, (samples, tile), 1) // rank
     for level in range(levels):
         width = 2**level
         half = p // width
@@ -198,10 +209,10 @@
                 sums = sums + abuf[start + i]
         else:
             sums = lax.fori_loop(1, width, lambda i, s, start=start: s + abuf[start + i], sums)
-        coefs.append(stacked(sums * (0.5 / (rank * width * sites) ** 0.5)))
-    low = dot(coefs[0], picked[0])
-    for level in range(1, levels):
-        low = low + dot(coefs[level], picked[level])
+        sums = sums * (0.5 / (rank * width * sites) ** 0.5)
+        coefs[level // side] = jnp.where(part_of == level % side, sums, coefs[level // side])
+    coefs = stacked(jnp.concatenate(coefs, axis=1)[:, :depth])
+    low = dot(coefs, picked)
     rbuf[:, at(p * slots, slots)] = at_slots - (low[:samples] + low[samples:])
     partners(lambda level, q: r_copy(q, p).start())
 
@@ -244,17 +255,20 @@
     if chunk < total:
         xbuf[...] = jnp.zeros_like(xbuf)
     loop(total // chunk, one_chunk)
-    xh, xl = split(xbuf[...])
+    xh, xl = split(xbuf[...].T)
+    lane = lax.broadcasted_iota(jnp.int32, (samples, pack * owned), 1)
+    mine = lane // owned == p % pack
+    xt[...] = jnp.concatenate([xh] * pack + [xl] * pack, axis=1)
 
     partners(lambda level, q: r_copy(q, q).wait_recv())
     rh, rl = split(rbuf[...])
-    both = dot_nt(jnp.concatenate([rh, rl], axis=0), xh)
-    cbuf[p] = both[:samples] + both[samples:] + dot_nt(rh, xl)
+    both = dot(jnp.concatenate([rh, rl], axis=0), xt[...])
+    wide = pack * owned
+    mixed = both[:samples, :wide] + both[samples:, :wide] + both[:samples, wide:]
+    cbuf[p] = jnp.where(mine, mixed, 0.0)
     partners(lambda level, q: c_copy(q, p).start())
 
-    low = dot(coefs[0], basis_ref[0])
-    for level in range(1, levels):
-        low = low + dot(coefs[level], basis_ref[level])
+    low = dot(coefs, basis)
     out_ref[...] = field + (low[:samples] + low[samples:])
 
     def one_tile(c):
@@ -280,19 +294,15 @@
     peers(lambda g: i_copy(g, o).wait_send())
     partners(lambda level, q: c_copy(q, q).wait_recv())
 
-    def correct(q):
-        coef = stacked(cbuf[q])
-        lines = at(q * owned, owned)
-        twice = dot(coef, kh[lines, :])
-        return twice[:samples] + twice[samples:] + dot(coef[:samples], kl[lines, :])
-
-    if leaves <= UNROLL:
-        total_sum = correct(0)
-        for q in range(1, leaves):
-            total_sum = total_sum + correct(q)
-    else:
-        total_sum = lax.fori_loop(1, leaves, lambda q, s: s + correct(q), correct(0))
-    out_ref[...] += total_sum
+    shares = []
+    for first_leaf in range(0, leaves, pack):
+        share = cbuf[first_leaf]
+        for q in range(first_leaf + 1, first_leaf + pack):
+            share = share + cbuf[q]
+        shares.append(share)
+    ch, cl = split(jnp.concatenate(shares, axis=1))
+    twice = dot(jnp.concatenate([ch, cl], axis=0), kh[...])
+    out_ref[...] += twice[:samples] + twice[samples:] + dot(ch, kl[...])
     partners(lambda level, q: c_copy(q, p).wait_send())
 
 
@@ -304,6 +314,9 @@
     slots = obs_site.shape[0]
     rows, total = inverse_rows.shape
     owned = rows * groups
+    pack = max(1, min(leaves, 128 // owned))
+    tile = max(1, 128 // rank) * rank
+    tiles = pl.cdiv(levels * rank, tile)
     vmem = pl.BlockSpec(memory_space=pltpu.VMEM)
     hbm = pl.BlockSpec(memory_space=pltpu.HBM)
     f32, bf16 = jnp.float32, jnp.bfloat16
@@ -323,13 +336,14 @@
             pltpu.VMEM((1, slots), f32),
             pltpu.SMEM((1,), jnp.int32),
             pltpu.SemaphoreType.DMA((8,)),
-            pltpu.VMEM((levels, samples, rank), f32),
-            pltpu.VMEM((leaves, samples, rank), f32),
+            pltpu.VMEM((tiles, samples, tile), f32),
+            pltpu.VMEM((leaves, samples, tile), f32),
             pltpu.VMEM((leaves, MSG, slots), f32),
             pltpu.VMEM((owned, total), f32),
             pltpu.VMEM((samples, leaves * slots), f32),
-            pltpu.VMEM((leaves, samples, owned), f32),
+            pltpu.VMEM((leaves, samples, pack * owned), f32),
             pltpu.VMEM((owned, leaves * slots), f32),
+            pltpu.VMEM((leaves * slots, 2 * pack * owned), bf16),
             pltpu.VMEM((total, MSG), f32),
             pltpu.VMEM((total, sites), bf16),
             pltpu.VMEM((total, sites), bf16),
@@ -339,7 +353,7 @@
             leaf_sem, leaf_sem, leaf_sem, leaf_sem,
         ],
         compiler_params=pltpu.CompilerParams(
-            collective_id=0, has_side_effects=True, vmem_limit_bytes=40 * 2**20
+            collective_id=0, has_side_effects=True, vmem_limit_bytes=62 * 2**20
         ),
         cost_estimate=pl.CostEstimate(
             flops=2 * samples * sites * total * 4,

time: 24.7 us -> 21.8 us (0.88)
  local copies, waits for them, and re-layouts: 4.52 us -> 1.32 us
  Pallas kernels: 19.2 us -> 19.5 us
    unnamed x15 -> x1, local copies, waits for them, and re-layouts: 4.52 us -> 1.32 us
    pallas_call x1, Pallas kernels: 19.2 us -> 19.5 us  [body(): pl.pallas_call(functools.partial(kernel, leaves, groups), out_shape=jax.S...]
where the time goes in v3:
time: 21.8 us; the launch traced here: 21.5 us
  Pallas kernels  19.5 us (89%)
  local copies, waits for them, and re-layouts  1.32 us (6%)
  between operations  0.66 us (3%)
    pallas_call x1, Pallas kernels, body(): pl.pallas_call(functools.partial(kernel, leaves, groups), out_shape=jax.S...  19.5 us
    unnamed x1, local copies, waits for them, and re-layouts  1.32 us

profile of v3, /device:TPU:0, one launch (start us, length us, event | category | flops | bytes accessed | tf_op | source)
XLA Modules:
  0.0 21.5 jit_solution(6139614841671268501)
XLA Ops:
  0.7 19.5 %shard_map.82 = f32[16,256]{1,0:T(8,128)} custom-call(bf16[16,256]{1,0:T(8,128)(2,1)} %z_hbm.1, bf16[256,256]{1,0:T(8,128)(2,1)} %diag_hbm.1, bf16[3,64,256]{2,1,0:T(8,128)(2,1)} %basis_hbm.1, f32[2,256]{1,0:T(2,128)} %xy_hbm.1, s32[1,128]{1,0:T(1,128)} %bitcast.2, f32[1,128]{1,0:T(1,128)} %bitcast.3, s32[1]{0:T(128)S(6)} %copy.10.count_hbm, f32[16,512]{1,0:T(8,128)} %inv_hbm.1), custom_call_target="tpu_custom_call" | custom-call | flops 16777216 | bytes 131072 | tf_op jit(solution)/shard_map/pallas_call | solution.py:325
  20.2 1.3 %copy.11 = f32[16,256]{1,0:T(8,128)} copy(f32[16,256]{1,0:T(8,128)} %shard_map.82) | data formatting | bytes 32768

commit v4 on v3

--- a/solution.py
+++ b/solution.py
@@ -31,6 +31,29 @@
 def stacked(a):
     high, low = split(a)
     return jnp.concatenate([high, low], axis=0)
+
+
+def thirds(x, y):
+    row = lax.broadcasted_iota(jnp.int32, (MSG, x.shape[1]), 0)
+    coord = jnp.where(row < 3, x, y)
+    first = coord.astype(jnp.bfloat16).astype(jnp.float32)
+    second = (coord - first).astype(jnp.bfloat16).astype(jnp.float32)
+    part = jnp.where(row % 3 == 0, first, jnp.where(row % 3 == 1, second, coord - first - second))
+    return jnp.where(row < 6, part, 0.0).astype(jnp.bfloat16)
+
+
+def fold(twin):
+    half = twin.shape[0] // 2
+    left = lax.broadcasted_iota(jnp.int32, (half, twin.shape[1]), 1) < twin.shape[1] // 2
+    return jnp.where(left, twin[:half], twin[half:])
+
+
+def unfold(even, odd):
+    middle = even.shape[1] // 2
+    left = lax.broadcasted_iota(jnp.int32, even.shape, 1) < middle
+    upper = jnp.where(left, even, pltpu.roll(odd, middle, 1))
+    lower = jnp.where(left, pltpu.roll(even, middle, 1), odd)
+    return jnp.concatenate([upper, lower], axis=0)
 
 
 def loop(count, step):
@@ -101,10 +124,7 @@
     slots = site_ref.shape[1]
     rows, total = inv_hbm.shape
     owned = rows * groups
-    pack = max(1, min(leaves, 128 // owned))
     depth = levels * rank
-    side = max(1, 128 // rank)
-    tile = side * rank
 
     def partners(step):
         for level in reversed(range(levels)):
@@ -140,14 +160,13 @@
         )
 
     def a_copy(level, q, who):
-        return to_leaf(proj.at[level // side], abuf.at[who], a_send, a_recv, q, who)
+        return to_leaf(proj.at[level], abuf.at[who], a_send, a_recv, q, who)
 
     def m_copy(q, who):
         return to_leaf(mbuf.at[who], mbuf.at[who], m_send, m_recv, q, who)
 
     def r_copy(q, who):
-        part = rbuf.at[:, at(who * slots, slots)]
-        return to_leaf(part, part, r_send, r_recv, q, who)
+        return to_leaf(rbuf.at[who], rbuf.at[who], r_send, r_recv, q, who)
 
     def c_copy(q, who):
         return to_leaf(cbuf.at[who], cbuf.at[who], c_send, c_recv, q, who)
@@ -163,12 +182,10 @@
     loads[1].wait()
     z = z_ref[...]
     basis = basis_ref[...].reshape(depth, sites)
-    project = dot_nt(z, basis)
-    spare = proj.shape[0] * tile - depth
-    if spare:
-        project = jnp.concatenate([project, jnp.zeros((samples, spare), jnp.float32)], axis=1)
-    for i in range(proj.shape[0]):
-        proj[i] = project[:, i * tile : (i + 1) * tile]
+    twins = [basis_ref[level // 2] for level in range(2 * levels)]
+    project = dot_nt(z, jnp.concatenate(twins, axis=0))
+    for level in range(levels):
+        proj[level] = fold(project[:, level * 2 * rank : (level + 1) * 2 * rank])
 
     pl.semaphore_wait(barrier, leaves - 1 + groups - 1)
     partners(lambda level, q: a_copy(level, q, p).start())
@@ -178,17 +195,12 @@
         load.wait()
     pick = (lax.broadcasted_iota(jnp.int32, (sites, slots), 0) == site_ref[...]).astype(jnp.float32)
     pick = pick.astype(jnp.bfloat16)
-    row = lax.broadcasted_iota(jnp.int32, (MSG, sites), 0)
-    coord = jnp.where(row < 3, xy_ref[0:1, :], xy_ref[1:2, :])
-    first = coord.astype(jnp.bfloat16).astype(jnp.float32)
-    second = (coord - first).astype(jnp.bfloat16).astype(jnp.float32)
-    third = coord - first - second
-    part = jnp.where(row % 3 == 0, first, jnp.where(row % 3 == 1, second, third))
-    part = jnp.where(row < 6, part, 0.0).astype(jnp.bfloat16)
+    part = thirds(xy_ref[0:1, :], xy_ref[1:2, :])
     message = dot(part, pick)
     count = count_ref[0].astype(jnp.float32)
-    message = jnp.where(lax.broadcasted_iota(jnp.int32, (MSG, slots), 0) == 6, count, message)
-    mbuf[p] = message
+    mbuf[p, :, :slots] = message[0:1] + message[1:2] + message[2:3]
+    mbuf[p, :, slots : 2 * slots] = message[3:4] + message[4:5] + message[5:6]
+    mbuf[p, :, 2 * slots :] = jnp.full((1, slots), count)
     partners(lambda level, q: m_copy(q, p).start())
     for load in loads[5:]:
         load.wait()
@@ -197,8 +209,7 @@
     field = dot(z, diag_ref[...])
 
     partners(lambda level, q: a_copy(level, q, q).wait_recv())
-    coefs = [jnp.zeros((samples, tile), jnp.float32)] * proj.shape[0]
-    part_of = lax.broadcasted_iota(jnp.int32, (samples, tile), 1) // rank
+    coefs = []
     for level in range(levels):
         width = 2**level
         half = p // width
@@ -209,15 +220,16 @@
                 sums = sums + abuf[start + i]
         else:
             sums = lax.fori_loop(1, width, lambda i, s, start=start: s + abuf[start + i], sums)
-        sums = sums * (0.5 / (rank * width * sites) ** 0.5)
-        coefs[level // side] = jnp.where(part_of == level % side, sums, coefs[level // side])
+        coefs.append(sums * (0.5 / (rank * width * sites) ** 0.5))
+    coefs = coefs + coefs[-1:] * (levels % 2)
+    coefs = [unfold(coefs[i], coefs[i + 1]) for i in range(0, len(coefs), 2)]
     coefs = stacked(jnp.concatenate(coefs, axis=1)[:, :depth])
     low = dot(coefs, picked)
-    rbuf[:, at(p * slots, slots)] = at_slots - (low[:samples] + low[samples:])
+    rbuf[p] = at_slots - (low[:samples] + low[samples:])
     partners(lambda level, q: r_copy(q, p).start())
 
     partners(lambda level, q: m_copy(q, q).wait_recv())
-    counts = jnp.concatenate([mbuf[q, 6:7, :] for q in range(leaves)], axis=0)
+    counts = jnp.concatenate([mbuf[q, :, 2 * slots :] for q in range(leaves)], axis=0)
     below = lax.broadcasted_iota(jnp.int32, (leaves, leaves), 1) < lax.broadcasted_iota(
         jnp.int32, (leaves, leaves), 0
     )
@@ -241,7 +253,7 @@
                 xbuf[:, lanes] = wide
             else:
                 xbuf[:, lanes] += wide
-            places = dot_nt(here, mbuf[q].astype(jnp.bfloat16))
+            places = dot_nt(here, thirds(mbuf[q, :, :slots], mbuf[q, :, slots : 2 * slots]))
             lines = at(c * chunk, chunk)
             if isinstance(q, int) and q == 0:
                 sbuf[lines, :] = places
@@ -256,16 +268,14 @@
         xbuf[...] = jnp.zeros_like(xbuf)
     loop(total // chunk, one_chunk)
     xh, xl = split(xbuf[...].T)
-    lane = lax.broadcasted_iota(jnp.int32, (samples, pack * owned), 1)
-    mine = lane // owned == p % pack
-    xt[...] = jnp.concatenate([xh] * pack + [xl] * pack, axis=1)
+    xt[...] = jnp.concatenate([xh, xh, xl, xl], axis=1)
 
     partners(lambda level, q: r_copy(q, q).wait_recv())
-    rh, rl = split(rbuf[...])
+    rh, rl = split(jnp.concatenate([rbuf[q] for q in range(leaves)], axis=1))
     both = dot(jnp.concatenate([rh, rl], axis=0), xt[...])
-    wide = pack * owned
+    wide = 2 * owned
     mixed = both[:samples, :wide] + both[samples:, :wide] + both[:samples, wide:]
-    cbuf[p] = jnp.where(mine, mixed, 0.0)
+    cbuf[p] = fold(mixed)
     partners(lambda level, q: c_copy(q, p).start())
 
     low = dot(coefs, basis)
@@ -294,12 +304,7 @@
     peers(lambda g: i_copy(g, o).wait_send())
     partners(lambda level, q: c_copy(q, q).wait_recv())
 
-    shares = []
-    for first_leaf in range(0, leaves, pack):
-        share = cbuf[first_leaf]
-        for q in range(first_leaf + 1, first_leaf + pack):
-            share = share + cbuf[q]
-        shares.append(share)
+    shares = [unfold(cbuf[q], cbuf[q + 1]) for q in range(0, leaves, 2)]
     ch, cl = split(jnp.concatenate(shares, axis=1))
     twice = dot(jnp.concatenate([ch, cl], axis=0), kh[...])
     out_ref[...] += twice[:samples] + twice[samples:] + dot(ch, kl[...])
@@ -314,9 +319,6 @@
     slots = obs_site.shape[0]
     rows, total = inverse_rows.shape
     owned = rows * groups
-    pack = max(1, min(leaves, 128 // owned))
-    tile = max(1, 128 // rank) * rank
-    tiles = pl.cdiv(levels * rank, tile)
     vmem = pl.BlockSpec(memory_space=pltpu.VMEM)
     hbm = pl.BlockSpec(memory_space=pltpu.HBM)
     f32, bf16 = jnp.float32, jnp.bfloat16
@@ -336,14 +338,14 @@
             pltpu.VMEM((1, slots), f32),
             pltpu.SMEM((1,), jnp.int32),
             pltpu.SemaphoreType.DMA((8,)),
-            pltpu.VMEM((tiles, samples, tile), f32),
-            pltpu.VMEM((leaves, samples, tile), f32),
-            pltpu.VMEM((leaves, MSG, slots), f32),
+            pltpu.VMEM((levels, samples // 2, 2 * rank), f32),
+            pltpu.VMEM((leaves, samples // 2, 2 * rank), f32),
+            pltpu.VMEM((leaves, 1, 3 * slots), f32),
             pltpu.VMEM((owned, total), f32),
-            pltpu.VMEM((samples, leaves * slots), f32),
-            pltpu.VMEM((leaves, samples, pack * owned), f32),
+            pltpu.VMEM((leaves, samples, slots), f32),
+            pltpu.VMEM((leaves, samples // 2, 2 * owned), f32),
             pltpu.VMEM((owned, leaves * slots), f32),
-            pltpu.VMEM((leaves * slots, 2 * pack * owned), bf16),
+            pltpu.VMEM((leaves * slots, 4 * owned), bf16),
             pltpu.VMEM((total, MSG), f32),
             pltpu.VMEM((total, sites), bf16),
             pltpu.VMEM((total, sites), bf16),

time: 21.8 us -> 21.8 us (level)
  no operation moved by 1% of the time
where the time goes in v4:
time: 21.8 us; the launch traced here: 21.5 us
  Pallas kernels  19.5 us (89%)
  local copies, waits for them, and re-layouts  1.32 us (6%)
  between operations  0.66 us (3%)
    pallas_call x1, Pallas kernels, body(): pl.pallas_call(functools.partial(kernel, leaves, groups), out_shape=jax.S...  19.5 us
    unnamed x1, local copies, waits for them, and re-layouts  1.32 us

profile of v4, /device:TPU:0, one launch (start us, length us, event | category | flops | bytes accessed | tf_op | source)
XLA Modules:
  0.0 21.5 jit_solution(7959122901658412371)
XLA Ops:
  0.7 19.5 %shard_map.82 = f32[16,256]{1,0:T(8,128)} custom-call(bf16[16,256]{1,0:T(8,128)(2,1)} %z_hbm.1, bf16[256,256]{1,0:T(8,128)(2,1)} %diag_hbm.1, bf16[3,64,256]{2,1,0:T(8,128)(2,1)} %basis_hbm.1, f32[2,256]{1,0:T(2,128)} %xy_hbm.1, s32[1,128]{1,0:T(1,128)} %bitcast.2, f32[1,128]{1,0:T(1,128)} %bitcast.3, s32[1]{0:T(128)S(6)} %copy.10.count_hbm, f32[16,512]{1,0:T(8,128)} %inv_hbm.1), custom_call_target="tpu_custom_call" | custom-call | flops 16777216 | bytes 131072 | tf_op jit(solution)/shard_map/pallas_call | solution.py:327
  20.2 1.3 %copy.11 = f32[16,256]{1,0:T(8,128)} copy(f32[16,256]{1,0:T(8,128)} %shard_map.82) | data formatting | bytes 32768
